TPU v7x, 32 devices: a whole 2x2x4 slice. The times are simulated.
32 devices in a mesh: lon: 4 (over y, x), lat: 4 (over z), phys: 2 (over core).
Axes of the slice: x: 2, y: 2, z: 4, core: 2. Of those that a mesh axis runs over, the one named last changes fastest.
Arguments:
- tracers: float32 [5, 128, 16, 1024], P(None, 'phys', 'lat', 'lon'), may hold values from -6 to 6
- wind_field: float32 [2, 128, 16, 1024], P(None, 'phys', 'lat', 'lon'), may hold values from -0.3 to 0.3
- diffusivity: float32 [128, 16, 1024], P('phys', 'lat', 'lon'), may hold values from 0.03 to 0.2
- weight_in: bfloat16 [256, 5, 128], replicated, may hold values from -0.25 to 0.25
- bias_in: float32 [256], replicated, may hold values from -3 to 3
- weight_mid: bfloat16 [256, 256], replicated, may hold values from -0.375 to 0.375
- bias_mid: float32 [256], replicated, may hold values from -3 to 3
- weight_out: bfloat16 [5, 128, 256], replicated, may hold values from -0.375 to 0.375
- bias_out: float32 [5, 128], replicated, may hold values from -2 to 2
Outputs:
- new_tracers: float32 [5, 128, 16, 1024], P(None, 'phys', 'lat', 'lon')
All inputs are finite; a program needn't handle non-finite values.
Results may differ from a plain program's by a relative error of at most 0.0029.
Values may be sent and summed in bfloat16 or wider, within the bound.
A program may use at most 64 MiB of HBM per device.

v0:
```python
import jax
import jax.numpy as jnp
from jax import lax
from jax.sharding import PartitionSpec as P


def passed_along(block, axis, distance):
    devices = range(lax.axis_size(axis))
    route = [((i - distance) % len(devices), i) for i in devices]
    return lax.ppermute(block, axis, route)


def passed_along_2(value, axis, steps):
    count = lax.axis_size(axis)
    leading, last = (max(0, -steps), min(count, count - steps))
    return lax.ppermute(value, axis, [(source, source + steps) for source in range(leading, last)])


def advance(center, eastward, westward, northward, southward, wind_east, wind_north, diffuse):
    return (
        center
        - 0.5 * wind_east * (eastward - westward)
        - 0.5 * wind_north * (northward - southward)
        + diffuse * (eastward + westward + northward + southward - 4.0 * center)
    )


def substep(field, wind_field, diffusivity):
    from_east = passed_along(field[:, :, :, :1], "lon", -1)
    from_west = passed_along(field[:, :, :, -1:], "lon", 1)
    from_north = passed_along_2(field[:, :, :1, :], "lat", -1)
    from_south = passed_along_2(field[:, :, -1:, :], "lat", 1)
    padded_rows = jnp.concatenate([from_south, field, from_north], axis=2)
    padded_cols = jnp.concatenate([from_west, field, from_east], axis=3)
    northward = padded_rows[:, :, 2:, :]
    southward = padded_rows[:, :, :-2, :]
    eastward = padded_cols[:, :, :, 2:]
    westward = padded_cols[:, :, :, :-2]
    return advance(
        field, eastward, westward, northward, southward, wind_field[0], wind_field[1], diffusivity
    )


def shards(
    tracers, wind_field, diffusivity, weight_in, bias_in, weight_mid, bias_mid, weight_out, bias_out
):
    field_count = tracers.shape[0]
    lev_dev = tracers.shape[1]
    lat_rows = tracers.shape[2]
    lon_cols = tracers.shape[3]
    field = tracers
    for substep_index in range(2):
        field = substep(field, wind_field, diffusivity)
    hidden_width = weight_mid.shape[0]
    levels = weight_in.shape[2]
    columns = lat_rows * lon_cols
    x_own = field.astype(jnp.bfloat16).reshape(field_count, lev_dev, columns)
    x_full = lax.all_to_all(x_own, "phys", split_axis=2, concat_axis=1, tiled=True)
    column_count = x_full.shape[2]
    pre_first = jnp.dot(
        weight_in.reshape(hidden_width, field_count * levels),
        x_full.reshape(field_count * levels, column_count),
        preferred_element_type=jnp.float32,
    )
    act_first = jax.nn.silu(pre_first + bias_in[:, None]).astype(jnp.bfloat16)
    pre_second = (
        jnp.dot(weight_mid, act_first, preferred_element_type=jnp.float32) + bias_mid[:, None]
    )
    act_second = jax.nn.silu(pre_second).astype(jnp.bfloat16)
    projected = jnp.dot(
        weight_out.reshape(field_count * levels, hidden_width),
        act_second,
        preferred_element_type=jnp.float32,
    )
    tendency_cols = (projected + bias_out.reshape(field_count * levels)[:, None]).astype(
        jnp.bfloat16
    )
    tendency_cols = tendency_cols.reshape(field_count, levels, column_count)
    tendency = lax.all_to_all(tendency_cols, "phys", split_axis=1, concat_axis=2, tiled=True)
    return field + tendency.astype(jnp.float32).reshape(field.shape)


def solution(mesh):
    placed = (
        P(None, "phys", "lat", "lon"),
        P(None, "phys", "lat", "lon"),
        P("phys", "lat", "lon"),
        P(),
        P(),
        P(),
        P(),
        P(),
        P(),
    )
    return jax.shard_map(
        shards, mesh=mesh, in_specs=placed, out_specs=P(None, "phys", "lat", "lon"), check_vma=False
    )
```

profile of v0, /device:TPU:0, one launch (start us, length us, event | category | flops | bytes accessed | tf_op | source)
XLA Modules:
  0.0 70.6 jit_solution(7654303753203688416)
XLA Ops:
  0.0 3.4 %fusion.11 = (f32[5,64,1,256]{3,2,1,0:T(1,128)}, f32[5,64,1,256]{3,2,1,0:T(1,128)}) fusion(f32[5,64,4,256]{3,2,1,0:T(4,128)} %param.9), kind=kLoop, calls=%fused_computation.29 | loop fusion | bytes 1310720 | tf_op jit(solution)/shard_map/slice | solution.py:32
  3.4 1.3 %collective-permute-start.2 = (f32[5,64,1,256]{3,2,1,0:T(1,128)}, f32[5,64,1,256]{3,2,1,0:T(1,128)}, u32[]{:S(2)}, u32[]{:S(2)}) collective-permute-start(f32[5,64,1,256]{3,2,1,0:T(1,128)} %get-tuple-element.14), channel_id=1, source_target_pairs={{2,0},{4,2},{6,4},{3,1},{5,3},{7,5},{10,8},{12,10},{14,12},{11,9},... | collective-permute-start | bytes 983048 | tf_op jit(solution)/shard_map/ppermute | solution.py:16
  4.7 6.3 %collective-permute-start.3 = (f32[5,64,1,256]{3,2,1,0:T(1,128)}, f32[5,64,1,256]{3,2,1,0:T(1,128)}, u32[]{:S(2)}, u32[]{:S(2)}) collective-permute-start(f32[5,64,1,256]{3,2,1,0:T(1,128)} %get-tuple-element.13), channel_id=1, source_target_pairs={{0,2},{2,4},{4,6},{1,3},{3,5},{5,7},{8,10},{10,12},{12,14},{9,11},... | collective-permute-start | bytes 983048 | tf_op jit(solution)/shard_map/ppermute | solution.py:16
  11.7 2.9 %collective-permute-start = (f32[5,64,4,1]{1,2,3,0:T(4,128)S(1)}, f32[5,64,4,1]{1,2,3,0:T(4,128)S(1)}, u32[]{:S(2)}, u32[]{:S(2)}) collective-permute-start(f32[5,64,4,1]{1,2,3,0:T(4,128)S(1)} %copy.35), channel_id=1, source_target_pairs={{8,0},{16,8},{24,16},{0,24},{9,1},{17,9},{25,17},{1,25},{10,2},{18... | collective-permute-start | bytes 15368 | tf_op jit(solution)/shard_map/ppermute | solution.py:10
  14.9 1.2 %multiply_bitcast_fusion.1 = (f32[64,4,256]{2,1,0:T(4,128)S(1)}, f32[64,4,256]{2,1,0:T(4,128)S(1)}) fusion(f32[2,64,4,256]{3,2,1,0:T(4,128)} %param.10), kind=kLoop, calls=%fused_computation.23 | loop fusion | flops 131072 | bytes 1048576 | tf_op jit(solution)/shard_map/mul | solution.py:22
  16.1 1.1 %copy.18 = f32[5,64,4,1]{3,2,1,0:T(4,128)} copy(f32[5,64,4,1]{1,2,3,0:T(4,128)S(1)} %collective-permute-done) | data formatting | bytes 10240 | tf_op jit(solution)/shard_map/ppermute | solution.py:10
  17.3 2.3 %collective-permute-done.1 = f32[5,64,4,1]{1,2,3,0:T(4,128)S(1)} collective-permute-done((f32[5,64,4,1]{1,2,3,0:T(4,128)S(1)}, f32[5,64,4,1]{1,2,3,0:T(4,128)S(1)}, u32[]{:S(2)}, u32[]{:S(2)}) %collective-permute-start.1) | collective-permute-done | bytes 5152 | tf_op jit(solution)/shard_map/ppermute | solution.py:10
  19.5 1.1 %copy.20 = f32[5,64,4,1]{3,2,1,0:T(4,128)} copy(f32[5,64,4,1]{1,2,3,0:T(4,128)S(1)} %collective-permute-done.1) | data formatting | bytes 10240 | tf_op jit(solution)/shard_map/ppermute | solution.py:10
  20.7 4.3 %multiply_add_fusion.1 = f32[5,64,4,256]{3,2,1,0:T(4,128)S(1)} fusion(f32[5,64,4,256]{3,2,1,0:T(4,128)S(1)} %copy-done.1, f32[5,64,1,256]{3,2,1,0:T(1,128)} %collective-permute-done.2, f32[5,64,1,256]{3,2,1,0:T(1,128)} %collective-permute-done.3, f32[5,64,4,1]{3,2,1,0:T(4,128)} %copy.18, f32[5,64,4,1]{3,2,1,0:T(4,128)} %copy.20, f32[64,4,256]{2,1,0:T(4,128)} %param.11, ...), kind=kLoop, calls=%fused_computation.12 | loop fusion | flops 5570560 | bytes 4073472 | tf_op jit(solution)/shard_map/add | solution.py:21
  25.0 1.3 %fusion.9 = (f32[5,64,1,256]{3,2,1,0:T(1,128)}, f32[5,64,1,256]{3,2,1,0:T(1,128)}) fusion(f32[5,64,4,256]{3,2,1,0:T(4,128)S(1)} %multiply_add_fusion.1), kind=kLoop, calls=%fused_computation.27 | loop fusion | bytes 1310720 | tf_op jit(solution)/shard_map/slice | solution.py:31
  26.3 1.3 %collective-permute-start.6 = (f32[5,64,1,256]{3,2,1,0:T(1,128)}, f32[5,64,1,256]{3,2,1,0:T(1,128)}, u32[]{:S(2)}, u32[]{:S(2)}) collective-permute-start(f32[5,64,1,256]{3,2,1,0:T(1,128)} %get-tuple-element.9), channel_id=1, source_target_pairs={{2,0},{4,2},{6,4},{3,1},{5,3},{7,5},{10,8},{12,10},{14,12},{11,9},... | collective-permute-start | bytes 983048 | tf_op jit(solution)/shard_map/ppermute | solution.py:16
  27.6 5.3 %collective-permute-start.7 = (f32[5,64,1,256]{3,2,1,0:T(1,128)}, f32[5,64,1,256]{3,2,1,0:T(1,128)}, u32[]{:S(2)}, u32[]{:S(2)}) collective-permute-start(f32[5,64,1,256]{3,2,1,0:T(1,128)} %get-tuple-element.10), channel_id=1, source_target_pairs={{0,2},{2,4},{4,6},{1,3},{3,5},{5,7},{8,10},{10,12},{12,14},{9,11},... | collective-permute-start | bytes 983048 | tf_op jit(solution)/shard_map/ppermute | solution.py:16
  34.7 1.2 %collective-permute-start.5 = (f32[5,64,4,1]{1,2,3,0:T(4,128)S(1)}, f32[5,64,4,1]{1,2,3,0:T(4,128)S(1)}, u32[]{:S(2)}, u32[]{:S(2)}) collective-permute-start(f32[5,64,4,1]{1,2,3,0:T(4,128)S(1)} %copy.23), channel_id=1, source_target_pairs={{24,0},{0,8},{8,16},{16,24},{25,1},{1,9},{9,17},{17,25},{26,2},{2,... | collective-permute-start | bytes 15368 | tf_op jit(solution)/shard_map/ppermute | solution.py:10
  36.0 1.9 %copy.28 = bf16[256,5,128]{0,2,1:T(8,128)(2,1)} copy(bf16[256,5,128]{2,0,1:T(8,128)(2,1)} %param.12) | data formatting | bytes 655360 | tf_op args[3]
  38.2 1.2 %collective-permute-done.5 = f32[5,64,4,1]{1,2,3,0:T(4,128)S(1)} collective-permute-done((f32[5,64,4,1]{1,2,3,0:T(4,128)S(1)}, f32[5,64,4,1]{1,2,3,0:T(4,128)S(1)}, u32[]{:S(2)}, u32[]{:S(2)}) %collective-permute-start.5) | collective-permute-done | bytes 5152 | tf_op jit(solution)/shard_map/ppermute | solution.py:10
  39.7 5.1 %fusion.7 = (bf16[5,64,4,256]{3,2,1,0:T(4,128)(2,1)}, f32[5,64,4,256]{3,2,1,0:T(4,128)}) fusion(f32[5,64,4,256]{3,2,1,0:T(4,128)S(1)} %multiply_add_fusion.1, f32[64,4,256]{2,1,0:T(4,128)} %param.11, f32[5,64,1,256]{3,2,1,0:T(1,128)} %collective-permute-done.7, f32[5,64,1,256]{3,2,1,0:T(1,128)} %collective-permute-done.6, ...), kind=kLoop, calls=%fused_computation.25 | loop fusion | flops 5898240 | bytes 4728832 | tf_op jit(solution)/shard_map/convert_element_type | solution.py:57
  44.8 2.5 %copy.33 = bf16[5,64,4,256]{1,0,3,2:T(8,128)(2,1)S(1)} copy(bf16[5,64,4,256]{3,2,1,0:T(4,128)(2,1)} %get-tuple-element.5) | data formatting | bytes 1310720 | tf_op jit(solution)/shard_map/reshape | solution.py:57
  47.4 1.3 %reshape.33 = bf16[2,2,81920]{2,1,0:T(2,128)(2,1)S(1)} reshape(bf16[1024,5,64]{2,1,0:T(8,128)(2,1)S(1)} %bitcast.36) | data formatting | bytes 1310720
  48.6 5.0 %all_to_all.24 = bf16[2,2,81920]{2,1,0:T(2,128)(2,1)} all-to-all(bf16[2,2,81920]{2,1,0:T(2,128)(2,1)S(1)} %reshape.33), channel_id=1, replica_groups=mesh['lon'=4,'lat'=4,'phys'=2] {'phys'}, dimensions={0} | all-to-all | bytes 1310720 | tf_op jit(solution)/shard_map/all_to_all | solution.py:58
  53.7 2.3 %reshape.34 = bf16[1024,5,64]{2,1,0:T(8,128)(2,1)S(1)} reshape(bf16[2,2,81920]{2,1,0:T(2,128)(2,1)} %all_to_all.24) | data formatting | bytes 1310720
  55.9 1.5 %copy.34 = bf16[5,64,2,512]{3,2,1,0:T(2,128)(2,1)S(1)} copy(bf16[5,64,2,512]{1,0,3,2:T(8,128)(2,1)S(1)} %bitcast.37) | data formatting | bytes 1310720 | tf_op jit(solution)/shard_map/all_to_all | solution.py:58
  60.6 4.6 %all_to_all.25 = bf16[5,128,512]{2,0,1:T(8,128)(2,1)S(1)} all-to-all(bf16[5,128,512]{2,0,1:T(8,128)(2,1)S(1)} %copy.30), channel_id=1, replica_groups=mesh['lon'=4,'lat'=4,'phys'=2] {'phys'}, dimensions={1} | all-to-all | bytes 1310720 | tf_op jit(solution)/shard_map/all_to_all | solution.py:79
  66.6 1.3 %reshape.31 = f32[5,64,4,256]{3,2,1,0:T(4,128)S(1)} reshape(f32[5,64,2,512]{3,2,1,0:T(2,128)S(1)} %copy.32) | data formatting | bytes 2621440 | tf_op jit(solution)/shard_map/convert_element_type | solution.py:80
  67.9 2.7 %add.86 = f32[5,64,4,256]{3,2,1,0:T(4,128)} add(f32[5,64,4,256]{3,2,1,0:T(4,128)} %get-tuple-element.6, f32[5,64,4,256]{3,2,1,0:T(4,128)S(1)} %reshape.31) | non-fusion elementwise | flops 327680 | bytes 3932160 | tf_op jit(solution)/shard_map/add | solution.py:80
  (38 shorter events, 7.9 us)
Async XLA Ops:
  0.0 58.9 %copy-start = (bf16[5,128,256]{2,1,0:T(8,128)(2,1)S(1)}, bf16[5,128,256]{2,1,0:T(8,128)(2,1)}, u32[]{:S(2)}) copy-start(bf16[5,128,256]{2,1,0:T(8,128)(2,1)} %param.16) | copy-start | bytes 983044
  0.0 11.0 %copy-start.1 = (f32[5,64,4,256]{3,2,1,0:T(4,128)S(1)}, f32[5,64,4,256]{3,2,1,0:T(4,128)}, u32[]{:S(2)}) copy-start(f32[5,64,4,256]{3,2,1,0:T(4,128)} %param.9) | copy-start | bytes 3932164
  3.4 17.2 %collective-permute-start.2 = (f32[5,64,1,256]{3,2,1,0:T(1,128)}, f32[5,64,1,256]{3,2,1,0:T(1,128)}, u32[]{:S(2)}, u32[]{:S(2)}) collective-permute-start(f32[5,64,1,256]{3,2,1,0:T(1,128)} %get-tuple-element.14), channel_id=1, source_target_pairs={{2,0},{4,2},{6,4},{3,1},{5,3},{7,5},{10,8},{12,10},{14,12},{11,9},... | collective-permute-start | bytes 983048 | tf_op jit(solution)/shard_map/ppermute | solution.py:16
  4.7 15.9 %collective-permute-start.3 = (f32[5,64,1,256]{3,2,1,0:T(1,128)}, f32[5,64,1,256]{3,2,1,0:T(1,128)}, u32[]{:S(2)}, u32[]{:S(2)}) collective-permute-start(f32[5,64,1,256]{3,2,1,0:T(1,128)} %get-tuple-element.13), channel_id=1, source_target_pairs={{0,2},{2,4},{4,6},{1,3},{3,5},{5,7},{8,10},{10,12},{12,14},{9,11},... | collective-permute-start | bytes 983048 | tf_op jit(solution)/shard_map/ppermute | solution.py:16
  11.7 4.4 %collective-permute-start = (f32[5,64,4,1]{1,2,3,0:T(4,128)S(1)}, f32[5,64,4,1]{1,2,3,0:T(4,128)S(1)}, u32[]{:S(2)}, u32[]{:S(2)}) collective-permute-start(f32[5,64,4,1]{1,2,3,0:T(4,128)S(1)} %copy.35), channel_id=1, source_target_pairs={{8,0},{16,8},{24,16},{0,24},{9,1},{17,9},{25,17},{1,25},{10,2},{18... | collective-permute-start | bytes 15368 | tf_op jit(solution)/shard_map/ppermute | solution.py:10
  14.9 4.6 %collective-permute-start.1 = (f32[5,64,4,1]{1,2,3,0:T(4,128)S(1)}, f32[5,64,4,1]{1,2,3,0:T(4,128)S(1)}, u32[]{:S(2)}, u32[]{:S(2)}) collective-permute-start(f32[5,64,4,1]{1,2,3,0:T(4,128)S(1)} %copy.36), channel_id=1, source_target_pairs={{24,0},{0,8},{8,16},{16,24},{25,1},{1,9},{9,17},{17,25},{26,2},{2,... | collective-permute-start | bytes 15368 | tf_op jit(solution)/shard_map/ppermute | solution.py:10
  26.3 13.4 %collective-permute-start.6 = (f32[5,64,1,256]{3,2,1,0:T(1,128)}, f32[5,64,1,256]{3,2,1,0:T(1,128)}, u32[]{:S(2)}, u32[]{:S(2)}) collective-permute-start(f32[5,64,1,256]{3,2,1,0:T(1,128)} %get-tuple-element.9), channel_id=1, source_target_pairs={{2,0},{4,2},{6,4},{3,1},{5,3},{7,5},{10,8},{12,10},{14,12},{11,9},... | collective-permute-start | bytes 983048 | tf_op jit(solution)/shard_map/ppermute | solution.py:16
  27.6 12.1 %collective-permute-start.7 = (f32[5,64,1,256]{3,2,1,0:T(1,128)}, f32[5,64,1,256]{3,2,1,0:T(1,128)}, u32[]{:S(2)}, u32[]{:S(2)}) collective-permute-start(f32[5,64,1,256]{3,2,1,0:T(1,128)} %get-tuple-element.10), channel_id=1, source_target_pairs={{0,2},{2,4},{4,6},{1,3},{3,5},{5,7},{8,10},{10,12},{12,14},{9,11},... | collective-permute-start | bytes 983048 | tf_op jit(solution)/shard_map/ppermute | solution.py:16
  33.6 4.2 %collective-permute-start.4 = (f32[5,64,4,1]{1,2,3,0:T(4,128)S(1)}, f32[5,64,4,1]{1,2,3,0:T(4,128)S(1)}, u32[]{:S(2)}, u32[]{:S(2)}) collective-permute-start(f32[5,64,4,1]{1,2,3,0:T(4,128)S(1)} %copy.21), channel_id=1, source_target_pairs={{8,0},{16,8},{24,16},{0,24},{9,1},{17,9},{25,17},{1,25},{10,2},{18... | collective-permute-start | bytes 15368 | tf_op jit(solution)/shard_map/ppermute | solution.py:10
  34.7 4.6 %collective-permute-start.5 = (f32[5,64,4,1]{1,2,3,0:T(4,128)S(1)}, f32[5,64,4,1]{1,2,3,0:T(4,128)S(1)}, u32[]{:S(2)}, u32[]{:S(2)}) collective-permute-start(f32[5,64,4,1]{1,2,3,0:T(4,128)S(1)} %copy.23), channel_id=1, source_target_pairs={{24,0},{0,8},{8,16},{16,24},{25,1},{1,9},{9,17},{17,25},{26,2},{2,... | collective-permute-start | bytes 15368 | tf_op jit(solution)/shard_map/ppermute | solution.py:10
  57.5 1.0 %copy-start.2 = (bf16[256,5,128]{0,2,1:T(8,128)(2,1)S(1)}, bf16[256,5,128]{0,2,1:T(8,128)(2,1)}, u32[]{:S(2)}) copy-start(bf16[256,5,128]{0,2,1:T(8,128)(2,1)} %copy.28) | copy-start | bytes 983044
  57.5 1.0 %copy-start.5 = (f32[256]{0:T(256)S(1)}, f32[256]{0:T(256)}, u32[]{:S(2)}) copy-start(f32[256]{0:T(256)} %param.13) | copy-start | bytes 3076
  58.4 0.9 %copy-start.3 = (bf16[256,256]{1,0:T(8,128)(2,1)S(1)}, bf16[256,256]{1,0:T(8,128)(2,1)}, u32[]{:S(2)}) copy-start(bf16[256,256]{1,0:T(8,128)(2,1)} %param.14) | copy-start | bytes 393220
  58.4 0.9 %copy-start.4 = (f32[5,128]{1,0:T(8,128)S(1)}, f32[5,128]{1,0:T(8,128)}, u32[]{:S(2)}) copy-start(f32[5,128]{1,0:T(8,128)} %param.17) | copy-start | bytes 7684
  58.4 0.9 %copy-start.6 = (f32[256]{0:T(256)S(1)}, f32[256]{0:T(256)}, u32[]{:S(2)}) copy-start(f32[256]{0:T(256)} %param.15) | copy-start | bytes 3076
where the time goes:
time: 71.1 us; the launch traced here: 70.6 us
  local copies, waits for them, and re-layouts  23.5 us (33%)
  starting transfers between devices  19.3 us (27%)
  other arithmetic  13.5 us (19%)
  blocking collectives  9.6 us (14%)
  waiting for transfers between devices  3.44 us (5%)
  matrix products  1.03 us (1%)
    ppermute x4, starting transfers between devices, passed_along_2(): lax.ppermute(value, axis, [(source, source + steps) for source in range(l...  14.2 us
    unnamed x19, local copies, waits for them, and re-layouts  7.25 us
    convert_element_type x1, other arithmetic, shards(): x_own = field.astype(jnp.bfloat16).reshape(field_count, lev_dev, columns)  5.15 us
    ppermute x4, starting transfers between devices, passed_along(): return lax.ppermute(block, axis, route)  5.1 us
    all_to_all x1, blocking collectives, shards(): lax.all_to_all(x_own, 'phys', split_axis=2, concat_axis=1, tiled=True)  5.03 us
    all_to_all x1, blocking collectives, shards(): lax.all_to_all(tendency_cols, 'phys', split_axis=1, concat_axis=2, tiled=...  4.58 us
    add x1, other arithmetic, advance(): center - 0.5 * wind_east * (eastward - westward)  4.31 us
    ppermute x4, waiting for transfers between devices, passed_along(): return lax.ppermute(block, axis, route)  3.43 us
  transfers between devices with their start and end apart: 8, of which 2 were waited for; matrix products, arithmetic and copies ran while one was open for 11% of the time, Pallas kernels for 0%

commit v1 on v0

v1 whole, which is shorter than its diff:
```python
import functools

import jax
import jax.numpy as jnp
from jax import lax
from jax.experimental import pallas as pl
from jax.experimental.pallas import tpu as pltpu
from jax.sharding import PartitionSpec as P

LANES = 128
BLK = 16
MESH = pl.DeviceIdType.MESH
f32, bf16 = jnp.float32, jnp.bfloat16


def silu(z):
    half = 0.5 * z
    return half + half * jnp.tanh(half)


def kernel(
    dims, tr_hbm, wind_hbm, diff_hbm, w1_hbm, b1_hbm, w2_hbm, b2_hbm, w3_hbm, b3_hbm, out_hbm,
    raw, wraw, draw, w1, w2, w3, b1r, b2r, b3r, b1, b2, b3,
    q0, q1, adv, cf, zs, zr, ls, lr, xb, oraw,
    in_sem, out_sem, zs_sem, zr_sem, ls_sem, lr_sem, xs_sem, xr_sem,
):
    F, L, R, C, H, LEV = dims
    tiles = C // LANES
    step_rows = tiles * R
    lon, lat, phys = (lax.axis_index(a) for a in ("lon", "lat", "phys"))
    nlon, nlat = lax.axis_size("lon"), lax.axis_size("lat")
    east, west = lax.rem(lon + 1, nlon), lax.rem(lon + nlon - 1, nlon)
    north, south = jnp.minimum(lat + 1, nlat - 1), jnp.maximum(lat - 1, 0)
    has_north, has_south = lat < nlat - 1, lat > 0
    other = 1 - phys
    own = pl.multiple_of(phys * L, L)

    loads = [pltpu.make_async_copy(
        tr_hbm.at[pl.ds(f * L * step_rows, L * step_rows)],
        raw.at[pl.ds(f * L * step_rows, L * step_rows)], in_sem.at[f]) for f in range(F)]
    pairs = [(wind_hbm, wraw), (diff_hbm, draw), (b1_hbm, b1r), (b2_hbm, b2r), (b3_hbm, b3r), (w2_hbm, w2)]
    pairs += [(w1_hbm.at[f], w1.at[:, pl.ds(f * LEV, LEV)]) for f in range(F)]
    pairs += [(w3_hbm.at[f, pl.ds(own, L)], w3.at[pl.ds(f * L, L)]) for f in range(F)]
    loads += [pltpu.make_async_copy(s, d, in_sem.at[F + k]) for k, (s, d) in enumerate(pairs)]
    for copy in loads:
        copy.start()

    barrier = pltpu.get_barrier_semaphore()
    for d in ({"lon": east}, {"lon": west}, {"phys": other}):
        pl.semaphore_signal(barrier, inc=1, device_id=d, device_id_type=MESH)

    @pl.when(has_north)
    def _():
        pl.semaphore_signal(barrier, inc=1, device_id={"lat": north}, device_id_type=MESH)

    @pl.when(has_south)
    def _():
        pl.semaphore_signal(barrier, inc=1, device_id={"lat": south}, device_id_type=MESH)

    def lat_copy(rnd, side, f):
        return pltpu.make_async_remote_copy(
            src_ref=zs.at[rnd, side, f], dst_ref=zr.at[rnd, side, f],
            send_sem=zs_sem.at[rnd, side, f], recv_sem=zr_sem.at[rnd, side, f],
            device_id={"lat": south if side else north}, device_id_type=MESH)

    def lon_copy(m, side):
        return pltpu.make_async_remote_copy(
            src_ref=ls.at[m, side], dst_ref=lr.at[m, side],
            send_sem=ls_sem.at[m, side], recv_sem=lr_sem.at[m, side],
            device_id={"lon": west if side else east}, device_id_type=MESH)

    def x_copy(ph, f):
        rows = pl.ds(pl.multiple_of(f * LEV + phys * L, L), L)
        return pltpu.make_async_remote_copy(
            src_ref=xb.at[ph, :, rows], dst_ref=xb.at[ph, :, rows],
            send_sem=xs_sem.at[ph, f], recv_sem=xr_sem.at[ph, f],
            device_id={"phys": other}, device_id_type=MESH)

    can_send = (has_north, has_south)
    can_recv = (has_south, has_north)

    def lat_start(rnd, f):
        for side in range(2):
            @pl.when(can_send[side])
            def _():
                lat_copy(rnd, side, f).start()

    def lat_wait(rnd, f):
        for side in range(2):
            @pl.when(can_recv[side])
            def _():
                lat_copy(rnd, side, f).wait_recv()

    for side, there in enumerate(can_recv):
        @pl.when(jnp.logical_not(there))
        def _():
            zr[:, side] = jnp.zeros(zr.shape[:1] + zr.shape[2:], bf16)

    lane = lax.broadcasted_iota(jnp.int32, (BLK, LANES), 1)
    wide = lax.broadcasted_iota(jnp.int32, (BLK, C), 1)

    def blocks(body):
        def run(k, carry):
            body(pl.ds(pl.multiple_of(k * BLK, BLK), BLK), k * BLK)
            return carry
        lax.fori_loop(0, L // BLK, run, 0)

    def spaced(f, r, level, t):
        return pl.ds(((f * L + level) * tiles + t) * R + r, BLK, stride=step_rows)

    def natural(ref, f, r, level):
        return jnp.concatenate([ref[spaced(f, r, level, t), :] for t in range(tiles)], axis=1)

    def pack(q, rows, m):
        def body(lev, _):
            to_east = jnp.zeros((BLK, LANES), f32)
            to_west = jnp.zeros((BLK, LANES), f32)
            for f in range(F):
                for r in rows:
                    j = f * R + r
                    last = q[f, r, lev, C - LANES:]
                    first = q[f, r, lev, :LANES]
                    to_east = jnp.where(lane == j, jnp.broadcast_to(last[:, LANES - 1:], (BLK, LANES)), to_east)
                    to_west = jnp.where(lane == j, jnp.broadcast_to(first[:, :1], (BLK, LANES)), to_west)
            ls[m, 0, lev, :] = to_east.astype(bf16)
            ls[m, 1, lev, :] = to_west.astype(bf16)
        blocks(body)
        for side in range(2):
            lon_copy(m, side).start()

    def stencil(q, f, r, lev, rnd, m):
        j = f * R + r
        c = q[f, r, lev, :]
        hw = lr[m, 0, lev, :].astype(f32)[:, j:j + 1]
        he = lr[m, 1, lev, :].astype(f32)[:, j:j + 1]
        w = jnp.where(wide == 0, jnp.broadcast_to(hw, (BLK, C)), pltpu.roll(c, 1, 1))
        e = jnp.where(wide == C - 1, jnp.broadcast_to(he, (BLK, C)), pltpu.roll(c, C - 1, 1))
        s = q[f, r - 1, lev, :] if r else zr[rnd, 0, f, lev, :].astype(f32)
        n = q[f, r + 1, lev, :] if r < R - 1 else zr[rnd, 1, f, lev, :].astype(f32)
        return (cf[0, r, lev, :] * c + cf[1, r, lev, :] * e + cf[2, r, lev, :] * w
                + cf[3, r, lev, :] * n + cf[4, r, lev, :] * s)

    edge, inner = (0, R - 1), tuple(range(1, R - 1))
    phases = (inner, edge)

    for f in range(F):
        loads[f].wait()

        def body(lev, level):
            for r in range(R):
                v = natural(raw, f, r, level)
                q0[f, r, lev, :] = v
                if r == R - 1:
                    zs[0, 0, f, lev, :] = v.astype(bf16)
                if r == 0:
                    zs[0, 1, f, lev, :] = v.astype(bf16)
        blocks(body)

    pl.semaphore_wait(barrier, 3 + has_north.astype(jnp.int32) + has_south.astype(jnp.int32))
    for f in range(F):
        lat_start(0, f)
    pack(q0, range(R), 0)

    for copy in loads[F:]:
        copy.wait()

    def coefficients(lev, level):
        for r in range(R):
            u = 0.5 * natural(wraw, 0, r, level)
            v = 0.5 * natural(wraw, 1, r, level)
            nu = natural(draw, 0, r, level)
            cf[0, r, lev, :] = 1.0 - 4.0 * nu
            cf[1, r, lev, :] = nu - u
            cf[2, r, lev, :] = nu + u
            cf[3, r, lev, :] = nu - v
            cf[4, r, lev, :] = nu + v
    blocks(coefficients)

    def columns(row):
        return jnp.transpose(jnp.broadcast_to(row, (LANES, LANES)))

    for k in range(H // LANES):
        b1[k * LANES:(k + 1) * LANES, :] = columns(b1r[k:k + 1, :])
        b2[k * LANES:(k + 1) * LANES, :] = columns(b2r[k:k + 1, :])
    for f in range(F):
        b3[f] = columns(b3r[f:f + 1, :])

    for side in range(2):
        lon_copy(0, side).wait_recv()

    def first_inner(lev, level):
        for r in inner:
            for f in range(F):
                q1[f, r, lev, :] = stencil(q0, f, r, lev, 0, 0)
    blocks(first_inner)
    pack(q1, inner, 1)

    for f in range(F):
        lat_wait(0, f)

        def first_edge(lev, level):
            for side, r in ((1, 0), (0, R - 1)):
                v = stencil(q0, f, r, lev, 0, 0)
                q1[f, r, lev, :] = v
                zs[1, side, f, lev, :] = v.astype(bf16)
        blocks(first_edge)
        lat_start(1, f)
    pack(q1, edge, 2)

    def second(f, ph, m):
        def body(lev, level):
            for i, r in enumerate(phases[ph]):
                v = stencil(q1, f, r, lev, 1, m)
                adv[ph, i, f, lev, :] = v
                xb[ph, i, pl.ds(pl.multiple_of(f * LEV + phys * L + level, BLK), BLK), :] = v.astype(bf16)
        blocks(body)
        x_copy(ph, f).start()

    def bias(ref):
        return jnp.concatenate([ref] * tiles, axis=1)

    def physics(ph):
        for i, r in enumerate(phases[ph]):
            pre = jnp.dot(w1[...], xb[ph, i], preferred_element_type=f32)
            act = silu(pre + bias(b1[...])).astype(bf16)
            pre = jnp.dot(w2[...], act, preferred_element_type=f32)
            act = silu(pre + bias(b2[...])).astype(bf16)
            for f in range(F):
                proj = jnp.dot(w3[f * L:(f + 1) * L, :], act, preferred_element_type=f32)
                ten = (proj + bias(b3[f, pl.ds(own, L), :])).astype(bf16).astype(f32)
                res = adv[ph, i, f] + ten
                for t in range(tiles):
                    oraw[pl.ds((f * L * tiles + t) * R + r, L, stride=step_rows), :] = (
                        res[:, t * LANES:(t + 1) * LANES])

    for side in range(2):
        lon_copy(1, side).wait_recv()
    for f in range(F):
        second(f, 0, 1)
    for f in range(F):
        x_copy(0, f).wait_recv()
    physics(0)

    for side in range(2):
        lon_copy(2, side).wait_recv()
    for f in range(F):
        lat_wait(1, f)
        second(f, 1, 2)
    for f in range(F):
        x_copy(1, f).wait_recv()
    physics(1)

    out = pltpu.make_async_copy(oraw, out_hbm, out_sem)
    out.start()
    for f in range(F):
        for rnd in range(2):
            for side in range(2):
                @pl.when(can_send[side])
                def _():
                    lat_copy(rnd, side, f).wait_send()
            x_copy(rnd, f).wait_send()
    for m in range(3):
        for side in range(2):
            lon_copy(m, side).wait_send()
    out.wait()


def as_stored(a, tiles):
    lead, rows = a.shape[:-2], a.shape[-2]
    a = a.reshape(lead + (rows, tiles, LANES))
    return jnp.swapaxes(a, -3, -2).reshape(-1, LANES)


def shards(tracers, wind_field, diffusivity, weight_in, bias_in, weight_mid, bias_mid, weight_out, bias_out):
    F, L, R, C = tracers.shape
    H, _, LEV = weight_in.shape
    tiles = C // LANES
    n = tracers.size // LANES
    dma = pltpu.SemaphoreType.DMA
    V = pltpu.VMEM
    out = pl.pallas_call(
        functools.partial(kernel, (F, L, R, C, H, LEV)),
        out_shape=jax.ShapeDtypeStruct((n, LANES), f32),
        in_specs=[pl.BlockSpec(memory_space=pl.ANY)] * 9,
        out_specs=pl.BlockSpec(memory_space=pl.ANY),
        scratch_shapes=[
            V((n, LANES), f32), V((2 * n // F, LANES), f32), V((n // F, LANES), f32),
            V((H, F * LEV), bf16), V((H, H), bf16), V((F * L, H), bf16),
            V((H // LANES, LANES), f32), V((H // LANES, LANES), f32), V((F, LEV), f32),
            V((H, LANES), f32), V((H, LANES), f32), V((F, LEV, LANES), f32),
            V((F, R, L, C), f32), V((F, R, L, C), f32), V((2, 2, F, L, C), f32), V((5, R, L, C), f32),
            V((2, 2, F, L, C), bf16), V((2, 2, F, L, C), bf16),
            V((3, 2, L, LANES), bf16), V((3, 2, L, LANES), bf16),
            V((2, 2, F * LEV, C), bf16), V((n, LANES), f32),
            dma((3 * F + 6,)), dma, dma((2, 2, F)), dma((2, 2, F)), dma((3, 2)), dma((3, 2)),
            dma((2, F)), dma((2, F)),
        ],
        compiler_params=pltpu.CompilerParams(
            collective_id=0, has_side_effects=True, vmem_limit_bytes=40 * 2**20),
    )(
        as_stored(tracers, tiles), as_stored(wind_field, tiles), as_stored(diffusivity, tiles),
        jnp.swapaxes(weight_in, 0, 1), bias_in.reshape(-1, LANES), weight_mid,
        bias_mid.reshape(-1, LANES), weight_out, bias_out,
    )
    out = out.reshape(F, L, tiles, R, LANES)
    return jnp.swapaxes(out, 2, 3).reshape(F, L, R, C)


def solution(mesh):
    placed = (
        P(None, "phys", "lat", "lon"), P(None, "phys", "lat", "lon"), P("phys", "lat", "lon"),
        P(), P(), P(), P(), P(), P(),
    )
    return jax.shard_map(
        shards, mesh=mesh, in_specs=placed, out_specs=P(None, "phys", "lat", "lon"), check_vma=False
    )
```

time: 71.1 us -> 32.2 us (0.45)
  Pallas kernels: 0 us -> 22.5 us
  starting transfers between devices: 19.3 us -> 0 us
  local copies, waits for them, and re-layouts: 23.5 us -> 9.26 us
  other arithmetic: 13.5 us -> 0 us
  blocking collectives: 9.6 us -> 0 us
  waiting for transfers between devices: 3.44 us -> 0 us
  matrix products: 1.03 us -> 0 us
    pallas_call x0 -> x1, Pallas kernels: none -> 22.5 us  [shards(): pl.pallas_call(functools.partial(kernel, (F, L, R, C, H, LEV)), out_shape...]
    ppermute x8 -> x0, starting transfers between devices: 19.3 us -> none  [the longest x4 14.2 us: passed_along_2(): lax.ppermute(value, axis, [(source, source + steps) for source in range(l...]
    all_to_all x2 -> x0, blocking collectives: 9.6 us -> none  [the longest x1 5.03 us: shards(): lax.all_to_all(x_own, 'phys', split_axis=2, concat_axis=1, tiled=True)]
    add x2 -> x0, other arithmetic: 7.02 us -> none  [the longest x1 4.31 us: advance(): center - 0.5 * wind_east * (eastward - westward)]
    slice x6 -> x0, local copies, waits for them, and re-layouts: 6.12 us -> none  [the longest x1 3.42 us: substep(): from_south = passed_along_2(field[:, :, -1:, :], 'lat', 1)]
    convert_element_type x2 -> x0, other arithmetic: 5.3 us -> none  [the longest x1 5.15 us: shards(): x_own = field.astype(jnp.bfloat16).reshape(field_count, lev_dev, columns)]
    ppermute x8 -> x0, waiting for transfers between devices: 3.44 us -> none  [the longest x4 3.43 us: passed_along(): return lax.ppermute(block, axis, route)]
    ppermute x4 -> x0, local copies, waits for them, and re-layouts: 2.9 us -> none  [passed_along(): return lax.ppermute(block, axis, route)]
  transfers between devices with their start and end apart: 8 -> 0, of which waited for: 2 -> 0; matrix products, arithmetic and copies ran while one was open for 11% -> 0% of each run, Pallas kernels for 0% -> 0%
where the time goes in v1:
time: 32.2 us; the launch traced here: 31.8 us
  Pallas kernels  22.5 us (70%)
  local copies, waits for them, and re-layouts  9.26 us (29%)
    pallas_call x1, Pallas kernels, shards(): pl.pallas_call(functools.partial(kernel, (F, L, R, C, H, LEV)), out_shape...  22.5 us
    unnamed x19, local copies, waits for them, and re-layouts  9.26 us

profile of v1, /device:TPU:0, one launch (start us, length us, event | category | flops | bytes accessed | tf_op | source)
XLA Modules:
  0.0 31.8 jit_solution(8044773000863181895)
XLA Ops:
  0.0 0.0 copy-start
  0.0 1.3 %copy-done = f32[5,64,4,256]{3,2,1,0:T(4,128)S(1)} copy-done((f32[5,64,4,256]{3,2,1,0:T(4,128)S(1)}, f32[5,64,4,256]{3,2,1,0:T(4,128)}, u32[]{:S(2)}) %copy-start) | copy-done | bytes 1310744
  1.3 0.0 copy-start.1
  1.3 1.0 %copy-done.1 = f32[2,64,4,256]{3,2,1,0:T(4,128)S(1)} copy-done((f32[2,64,4,256]{3,2,1,0:T(4,128)S(1)}, f32[2,64,4,256]{3,2,1,0:T(4,128)}, u32[]{:S(2)}) %copy-start.1) | copy-done | bytes 524312
  2.4 0.0 copy-start.2
  2.4 1.0 %copy-done.2 = bf16[256,5,128]{2,0,1:T(8,128)(2,1)S(1)} copy-done((bf16[256,5,128]{2,0,1:T(8,128)(2,1)S(1)}, bf16[256,5,128]{2,0,1:T(8,128)(2,1)}, u32[]{:S(2)}) %copy-start.2) | copy-done | bytes 327704
  3.3 0.0 copy-start.3
  3.3 1.0 %copy-done.3 = bf16[5,128,256]{2,1,0:T(8,128)(2,1)S(1)} copy-done((bf16[5,128,256]{2,1,0:T(8,128)(2,1)S(1)}, bf16[5,128,256]{2,1,0:T(8,128)(2,1)}, u32[]{:S(2)}) %copy-start.3) | copy-done | bytes 327704
  4.3 0.0 copy-start.4
  4.3 0.9 %copy-done.4 = f32[64,4,256]{2,1,0:T(4,128)S(1)} copy-done((f32[64,4,256]{2,1,0:T(4,128)S(1)}, f32[64,4,256]{2,1,0:T(4,128)}, u32[]{:S(2)}) %copy-start.4) | copy-done | bytes 262168
  5.3 0.0 copy-start.5
  5.3 0.9 %copy-done.5 = bf16[256,256]{1,0:T(8,128)(2,1)S(1)} copy-done((bf16[256,256]{1,0:T(8,128)(2,1)S(1)}, bf16[256,256]{1,0:T(8,128)(2,1)}, u32[]{:S(2)}) %copy-start.5) | copy-done | bytes 131096
  6.2 0.0 copy-start.6
  6.2 0.7 %copy-done.6 = f32[5,128]{1,0:T(8,128)S(1)} copy-done((f32[5,128]{1,0:T(8,128)S(1)}, f32[5,128]{1,0:T(8,128)}, u32[]{:S(2)}) %copy-start.6) | copy-done | bytes 2584
  6.8 0.0 copy-start.7
  6.9 0.7 %copy-done.7 = f32[256]{0:T(256)S(1)} copy-done((f32[256]{0:T(256)S(1)}, f32[256]{0:T(256)}, u32[]{:S(2)}) %copy-start.7) | copy-done | bytes 1048
  7.5 0.0 copy-start.8
  7.5 0.7 %copy-done.8 = f32[256]{0:T(256)S(1)} copy-done((f32[256]{0:T(256)S(1)}, f32[256]{0:T(256)}, u32[]{:S(2)}) %copy-start.8) | copy-done | bytes 1048
  8.2 22.5 %shard_map.91 = f32[2560,128]{1,0:T(8,128)S(1)} custom-call(f32[2560,128]{1,0:T(8,128)S(1)} %bitcast.24, f32[1024,128]{1,0:T(8,128)S(1)} %bitcast.25, f32[512,128]{1,0:T(8,128)S(1)} %bitcast.27, bf16[5,256,128]{2,1,0:T(8,128)(2,1)S(1)} %bitcast.26, f32[2,128]{1,0:T(2,128)S(1)} %bitcast.28, bf16[256,256]{1,0:T(8,128)(2,1)S(1)} %copy-done.5, ...), custom_call_target="tpu_custom_call" | custom-call | tf_op jit(solution)/shard_map/pallas_call | solution.py:281
  30.7 1.1 %copy.15 = f32[5,64,4,256]{3,2,1,0:T(4,128)} copy(f32[5,64,4,256]{3,2,1,0:T(4,128)S(1)} %bitcast.23) | data formatting | bytes 2621440
Async XLA Ops:
  0.0 1.3 %copy-start = (f32[5,64,4,256]{3,2,1,0:T(4,128)S(1)}, f32[5,64,4,256]{3,2,1,0:T(4,128)}, u32[]{:S(2)}) copy-start(f32[5,64,4,256]{3,2,1,0:T(4,128)} %param.9) | copy-start | bytes 3932164
  1.3 1.0 %copy-start.1 = (f32[2,64,4,256]{3,2,1,0:T(4,128)S(1)}, f32[2,64,4,256]{3,2,1,0:T(4,128)}, u32[]{:S(2)}) copy-start(f32[2,64,4,256]{3,2,1,0:T(4,128)} %param.10) | copy-start | bytes 1572868
  2.4 1.0 %copy-start.2 = (bf16[256,5,128]{2,0,1:T(8,128)(2,1)S(1)}, bf16[256,5,128]{2,0,1:T(8,128)(2,1)}, u32[]{:S(2)}) copy-start(bf16[256,5,128]{2,0,1:T(8,128)(2,1)} %param.12) | copy-start | bytes 983044
  3.3 1.0 %copy-start.3 = (bf16[5,128,256]{2,1,0:T(8,128)(2,1)S(1)}, bf16[5,128,256]{2,1,0:T(8,128)(2,1)}, u32[]{:S(2)}) copy-start(bf16[5,128,256]{2,1,0:T(8,128)(2,1)} %w3_hbm.1) | copy-start | bytes 983044
  4.3 0.9 %copy-start.4 = (f32[64,4,256]{2,1,0:T(4,128)S(1)}, f32[64,4,256]{2,1,0:T(4,128)}, u32[]{:S(2)}) copy-start(f32[64,4,256]{2,1,0:T(4,128)} %param.11) | copy-start | bytes 786436
  5.3 0.9 %copy-start.5 = (bf16[256,256]{1,0:T(8,128)(2,1)S(1)}, bf16[256,256]{1,0:T(8,128)(2,1)}, u32[]{:S(2)}) copy-start(bf16[256,256]{1,0:T(8,128)(2,1)} %w2_hbm.1) | copy-start | bytes 393220
  6.2 0.7 %copy-start.6 = (f32[5,128]{1,0:T(8,128)S(1)}, f32[5,128]{1,0:T(8,128)}, u32[]{:S(2)}) copy-start(f32[5,128]{1,0:T(8,128)} %b3_hbm.1) | copy-start | bytes 7684
  6.8 0.7 %copy-start.7 = (f32[256]{0:T(256)S(1)}, f32[256]{0:T(256)}, u32[]{:S(2)}) copy-start(f32[256]{0:T(256)} %param.13) | copy-start | bytes 3076
  7.5 0.7 %copy-start.8 = (f32[256]{0:T(256)S(1)}, f32[256]{0:T(256)}, u32[]{:S(2)}) copy-start(f32[256]{0:T(256)} %param.15) | copy-start | bytes 3076

commit v2 on v1

--- a/solution.py
+++ b/solution.py
@@ -19,10 +19,10 @@
 
 
 def kernel(
-    dims, tr_hbm, wind_hbm, diff_hbm, w1_hbm, b1_hbm, w2_hbm, b2_hbm, w3_hbm, b3_hbm, out_hbm,
+    dims, tr_hbm, wind_hbm, diff_hbm, w1_hbm, b1_hbm, w2_hbm, b2_hbm, w3_hbm, b3_hbm, oraw,
     raw, wraw, draw, w1, w2, w3, b1r, b2r, b3r, b1, b2, b3,
-    q0, q1, adv, cf, zs, zr, ls, lr, xb, oraw,
-    in_sem, out_sem, zs_sem, zr_sem, ls_sem, lr_sem, xs_sem, xr_sem,
+    q0, q1, adv, cf, zs, zr, ls, lr, xb,
+    in_sem, zs_sem, zr_sem, ls_sem, lr_sem, xs_sem, xr_sem,
 ):
     F, L, R, C, H, LEV = dims
     tiles = C // LANES
@@ -103,7 +103,7 @@
         def run(k, carry):
             body(pl.ds(pl.multiple_of(k * BLK, BLK), BLK), k * BLK)
             return carry
-        lax.fori_loop(0, L // BLK, run, 0)
+        lax.fori_loop(0, L // BLK, run, 0, unroll=True)
 
     def spaced(f, r, level, t):
         return pl.ds(((f * L + level) * tiles + t) * R + r, BLK, stride=step_rows)
@@ -250,8 +250,6 @@
         x_copy(1, f).wait_recv()
     physics(1)
 
-    out = pltpu.make_async_copy(oraw, out_hbm, out_sem)
-    out.start()
     for f in range(F):
         for rnd in range(2):
             for side in range(2):
@@ -262,7 +260,6 @@
     for m in range(3):
         for side in range(2):
             lon_copy(m, side).wait_send()
-    out.wait()
 
 
 def as_stored(a, tiles):
@@ -281,8 +278,8 @@
     out = pl.pallas_call(
         functools.partial(kernel, (F, L, R, C, H, LEV)),
         out_shape=jax.ShapeDtypeStruct((n, LANES), f32),
-        in_specs=[pl.BlockSpec(memory_space=pl.ANY)] * 9,
-        out_specs=pl.BlockSpec(memory_space=pl.ANY),
+        in_specs=[pl.BlockSpec(memory_space=pltpu.HBM)] * 9,
+        out_specs=pl.BlockSpec(memory_space=pltpu.VMEM),
         scratch_shapes=[
             V((n, LANES), f32), V((2 * n // F, LANES), f32), V((n // F, LANES), f32),
             V((H, F * LEV), bf16), V((H, H), bf16), V((F * L, H), bf16),
@@ -291,17 +288,17 @@
             V((F, R, L, C), f32), V((F, R, L, C), f32), V((2, 2, F, L, C), f32), V((5, R, L, C), f32),
             V((2, 2, F, L, C), bf16), V((2, 2, F, L, C), bf16),
             V((3, 2, L, LANES), bf16), V((3, 2, L, LANES), bf16),
-            V((2, 2, F * LEV, C), bf16), V((n, LANES), f32),
-            dma((3 * F + 6,)), dma, dma((2, 2, F)), dma((2, 2, F)), dma((3, 2)), dma((3, 2)),
+            V((2, 2, F * LEV, C), bf16),
+            dma((3 * F + 6,)), dma((2, 2, F)), dma((2, 2, F)), dma((3, 2)), dma((3, 2)),
             dma((2, F)), dma((2, F)),
         ],
         compiler_params=pltpu.CompilerParams(
-            collective_id=0, has_side_effects=True, vmem_limit_bytes=40 * 2**20),
-    )(
+            collective_id=0, has_side_effects=True, vmem_limit_bytes=32 * 2**20),
+    )(*(pltpu.with_memory_space_constraint(a, pltpu.HBM) for a in (
         as_stored(tracers, tiles), as_stored(wind_field, tiles), as_stored(diffusivity, tiles),
         jnp.swapaxes(weight_in, 0, 1), bias_in.reshape(-1, LANES), weight_mid,
         bias_mid.reshape(-1, LANES), weight_out, bias_out,
-    )
+    )))
     out = out.reshape(F, L, tiles, R, LANES)
     return jnp.swapaxes(out, 2, 3).reshape(F, L, R, C)
 

time: 32.2 us -> 20.4 us (0.63)
  local copies, waits for them, and re-layouts: 9.26 us -> 1.06 us
  Pallas kernels: 22.5 us -> 19.1 us
    unnamed x19 -> x1, local copies, waits for them, and re-layouts: 9.26 us -> 1.06 us
    pallas_call x1, Pallas kernels: 22.5 us -> 19.1 us  [shards(): pl.pallas_call(functools.partial(kernel, (F, L, R, C, H, LEV)), out_shape...]
where the time goes in v2:
time: 20.4 us; the launch traced here: 20.2 us
  Pallas kernels  19.1 us (94%)
  local copies, waits for them, and re-layouts  1.06 us (5%)
    pallas_call x1, Pallas kernels, shards(): pl.pallas_call(functools.partial(kernel, (F, L, R, C, H, LEV)), out_shape...  19.1 us
    unnamed x1, local copies, waits for them, and re-layouts  1.06 us

profile of v2, /device:TPU:0, one launch (start us, length us, event | category | flops | bytes accessed | tf_op | source)
XLA Modules:
  0.0 20.2 jit_solution(12214128036652678800)
XLA Ops:
  0.0 19.1 %shard_map.91 = f32[2560,128]{1,0:T(8,128)S(1)} custom-call(f32[2560,128]{1,0:T(8,128)} %bitcast.24, f32[1024,128]{1,0:T(8,128)} %bitcast.25, f32[512,128]{1,0:T(8,128)} %bitcast.27, bf16[5,256,128]{2,1,0:T(8,128)(2,1)} %bitcast.26, f32[2,128]{1,0:T(2,128)} %bitcast.28, bf16[256,256]{1,0:T(8,128)(2,1)} %w2_hbm.1, f32[2,128]{1,0:T(2,128)} %bitcast.29, ...), custom_call_target="tpu_custom_call" | custom-call | tf_op jit(solution)/shard_map/pallas_call | solution.py:278
  19.2 1.1 %copy.15 = f32[5,64,4,256]{3,2,1,0:T(4,128)} copy(f32[5,64,4,256]{3,2,1,0:T(4,128)S(1)} %bitcast.23) | data formatting | bytes 2621440

commit v3 on v2

--- a/solution.py
+++ b/solution.py
@@ -125,6 +125,8 @@
             ls[m, 0, lev, :] = to_east.astype(bf16)
             ls[m, 1, lev, :] = to_west.astype(bf16)
         blocks(body)
+
+    def lon_start(m):
         for side in range(2):
             lon_copy(m, side).start()
 
@@ -156,10 +158,11 @@
                     zs[0, 1, f, lev, :] = v.astype(bf16)
         blocks(body)
 
+    pack(q0, range(R), 0)
     pl.semaphore_wait(barrier, 3 + has_north.astype(jnp.int32) + has_south.astype(jnp.int32))
+    lon_start(0)
     for f in range(F):
         lat_start(0, f)
-    pack(q0, range(R), 0)
 
     for copy in loads[F:]:
         copy.wait()
@@ -194,6 +197,7 @@
                 q1[f, r, lev, :] = stencil(q0, f, r, lev, 0, 0)
     blocks(first_inner)
     pack(q1, inner, 1)
+    lon_start(1)
 
     for f in range(F):
         lat_wait(0, f)
@@ -206,6 +210,7 @@
         blocks(first_edge)
         lat_start(1, f)
     pack(q1, edge, 2)
+    lon_start(2)
 
     def second(f, ph, m):
         def body(lev, level):

time: 20.4 us -> 19.9 us (0.975)
  Pallas kernels: 19.1 us -> 18.7 us
    pallas_call x1, Pallas kernels: 19.1 us -> 18.7 us  [shards(): pl.pallas_call(functools.partial(kernel, (F, L, R, C, H, LEV)), out_shape...]
where the time goes in v3:
time: 19.9 us; the launch traced here: 19.8 us
  Pallas kernels  18.7 us (94%)
  local copies, waits for them, and re-layouts  1.06 us (5%)
    pallas_call x1, Pallas kernels, shards(): pl.pallas_call(functools.partial(kernel, (F, L, R, C, H, LEV)), out_shape...  18.7 us
    unnamed x1, local copies, waits for them, and re-layouts  1.06 us

profile of v3, /device:TPU:0, one launch (start us, length us, event | category | flops | bytes accessed | tf_op | source)
XLA Modules:
  0.0 19.8 jit_solution(3441393777627995543)
XLA Ops:
  0.0 18.7 %shard_map.91 = f32[2560,128]{1,0:T(8,128)S(1)} custom-call(f32[2560,128]{1,0:T(8,128)} %bitcast.24, f32[1024,128]{1,0:T(8,128)} %bitcast.25, f32[512,128]{1,0:T(8,128)} %bitcast.27, bf16[5,256,128]{2,1,0:T(8,128)(2,1)} %bitcast.26, f32[2,128]{1,0:T(2,128)} %bitcast.28, bf16[256,256]{1,0:T(8,128)(2,1)} %w2_hbm.1, f32[2,128]{1,0:T(2,128)} %bitcast.29, ...), custom_call_target="tpu_custom_call" | custom-call | tf_op jit(solution)/shard_map/pallas_call | solution.py:283
  18.7 1.1 %copy.15 = f32[5,64,4,256]{3,2,1,0:T(4,128)} copy(f32[5,64,4,256]{3,2,1,0:T(4,128)S(1)} %bitcast.23) | data formatting | bytes 2621440
